TPU v7x, 512 devices: a whole 4x4x16 slice. The times are simulated.
512 devices in a mesh: rep: 16 (over y, x_hi, core), fsdp: 32 (over x_lo, z).
Axes of the slice: x: 4 (x_hi: 2, x_lo: 2; x = x_hi * 2 + x_lo), y: 4, z: 16, core: 2. Of those that a mesh axis runs over, the one named last changes fastest.
Arguments:
- codes: int32 [16, 4194304], P('rep', 'fsdp'), may hold values from 0 to 15
- scales: float32 [16, 65536], P('rep', 'fsdp'), may hold values from 0.02 to 0.3
- base: float32 [4194304], P('fsdp'), may hold values from -6 to 6
- momentum: float32 [4194304], P('fsdp'), may hold values from -3 to 3
- inputs: bfloat16 [16, 4096, 8192], P('rep', 'fsdp'), may hold values from -30 to 30
- gain: bfloat16 [16, 8192], P('rep', 'fsdp'), may hold values from 0.099609375 to 1.8984375
- cotangent: bfloat16 [16, 4096, 512], P('rep', 'fsdp'), may hold values from -0.25 to 0.25
Outputs:
- new_base: float32 [4194304], P('fsdp')
- new_momentum: float32 [4194304], P('fsdp')
- keys: bfloat16 [16, 4096, 512], P('rep', 'fsdp')
- grad_weight: float32 [16, 8192, 512], P('rep', 'fsdp')
- grad_gain: float32 [16, 8192], P('rep', 'fsdp')
Inputs may be any that keep to these rules, and one draw needn't show every extreme that they name: `codes`: each entry is one 4-bit code.
All inputs are finite; a program needn't handle non-finite values.
Results may differ from a plain program's by a relative error of at most 0.015.
Values may be sent and summed in bfloat16 or wider, within the bound.
A program may use at most 64 MiB of HBM per device.

v0:
```python
import jax
import jax.numpy as jnp
from jax import lax
from jax.sharding import PartitionSpec as P

D = 8192
BLOCK = 64


outer_rate = 0.7
momentum_decay = 0.9


def shards(codes, scales, base, momentum, inputs, gain, cotangent):
    decoded = (codes[0] - 8).astype(jnp.float32) * jnp.repeat(scales[0], BLOCK)
    replicas = lax.axis_size("rep")
    average = lax.psum(decoded.astype(jnp.bfloat16), "rep").astype(jnp.float32) / replicas
    new_momentum = momentum_decay * momentum + average
    new_base = base - outer_rate * (average + momentum_decay * new_momentum)
    activations = inputs[0]
    upstream = cotangent[0]
    own_gain = gain[0]
    own_rows = own_gain.shape[0]
    tok_rows = activations.shape[0]
    key_width = upstream.shape[1]
    own_weight = (new_base.reshape(own_rows, key_width) * D ** (-0.5)).astype(jnp.bfloat16)
    contract_last = (((1,), (1,)), ((), ()))
    wide = activations.astype(jnp.float32)
    inv_rms = lax.rsqrt(jnp.mean(wide * wide, axis=1) + 1e-05)
    every_scale = lax.all_gather(inv_rms, "fsdp", axis=0, tiled=True)
    columns = lax.all_to_all(activations, "fsdp", split_axis=1, concat_axis=0, tiled=True)
    every_upstream = lax.all_gather(upstream, "fsdp", axis=0, tiled=True)
    scaled = columns.astype(jnp.float32) * every_scale[:, None]
    normed_cols = (scaled * own_gain.astype(jnp.float32)).astype(jnp.bfloat16)
    grad_rows = lax.dot_general(
        normed_cols, every_upstream, (((0,), (0,)), ((), ())), preferred_element_type=jnp.float32
    )
    back = lax.dot_general(
        every_upstream, own_weight, contract_last, preferred_element_type=jnp.float32
    )
    grad_total = jnp.sum(back * scaled, axis=0)
    weight_piece = lax.all_gather(own_weight, "fsdp", axis=0, tiled=True)
    gain_piece = lax.all_gather(own_gain, "fsdp", axis=0, tiled=True)
    count = weight_piece.shape[0]
    blocks = count // own_rows
    normed = (wide * inv_rms[:, None] * gain_piece.astype(jnp.float32)).astype(jnp.bfloat16)
    partial_value = jnp.einsum(
        "tgr,grk->gtk",
        normed.reshape(tok_rows, blocks, own_rows),
        weight_piece.reshape(blocks, own_rows, key_width),
        preferred_element_type=jnp.float32,
    )
    partial_value = lax.optimization_barrier(partial_value.astype(jnp.bfloat16)).astype(jnp.float32)
    key_total = jnp.sum(partial_value, axis=0)
    return (
        new_base,
        new_momentum,
        key_total.astype(jnp.bfloat16)[None],
        grad_rows[None],
        grad_total[None],
    )


def solution(mesh):
    placed = (
        P("rep", "fsdp"),
        P("rep", "fsdp"),
        P("fsdp"),
        P("fsdp"),
        P("rep", "fsdp", None),
        P("rep", "fsdp"),
        P("rep", "fsdp", None),
    )
    return jax.shard_map(
        shards,
        mesh=mesh,
        in_specs=placed,
        out_specs=(
            P("fsdp"),
            P("fsdp"),
            P("rep", "fsdp", None),
            P("rep", "fsdp", None),
            P("rep", "fsdp"),
        ),
        check_vma=False,
    )
```

profile of v0, /device:TPU:32, one launch (start us, length us, event | category | flops | bytes accessed | tf_op | source)
XLA Modules:
  0.0 448.1 jit_solution(13341294170569126215)
XLA Ops:
  8.0 0.0 copy-start
  8.0 0.0 all-reduce.2.cloned.1.call-start
  8.1 2.5 add_convert_fusion
  10.5 1.0 broadcast_in_dim.16
  11.5 1.0 reshape.51
  12.5 2.0 multiply_convert_fusion.7
  14.5 0.0 all-reduce.2.cloned.1.call-update
  14.6 0.0 all-gather.8.cloned.1.call-start
  14.6 0.5 all-gather.8.cloned.1.call-update
  15.1 0.0 all-gather.6.cloned.1.call-start
  15.2 156.8 %all-reduce.2.cloned.1.call-done = bf16[131072]{0:T(1024)(128)(2,1)} async-done(((bf16[131072]{0:T(1024)(128)(2,1)}), bf16[131072]{0:T(1024)(128)(2,1)}) %all-reduce.2.cloned.1.call-update) | async-done | bytes 262160 | tf_op jit(solution)/shard_map/psum | solution.py:17
  172.0 2.4 multiply_convert_fusion.6
  174.4 0.9 convert_element_type.57
  175.2 0.0 all-gather.6.cloned.1.call-update
  175.3 0.0 copy-done
  175.3 0.0 copy-start.2
  175.3 2.5 copy.16
  177.8 0.0 copy-start.1
  177.8 13.5 %all-to-all-start = ((bf16[128,32,256]{0,2,1:T(8,128)(2,1)}), bf16[128,32,256]{0,2,1:T(8,128)(2,1)}, u32[]{:S(2)}, u32[]{:S(2)}) async-start(bf16[128,32,256]{0,2,1:T(8,128)(2,1)} %bitcast.2), calls=%async_computation | async-start | bytes 4194304 | tf_op jit(solution)/shard_map/all_to_all | solution.py:31
  191.3 0.0 copy-done.2
  191.3 165.3 %all-gather = bf16[1,8192]{1,0:T(2,128)(2,1)S(1)} all-gather(bf16[1,256]{1,0:T(2,128)(2,1)S(1)} %copy-done.2), channel_id=2, replica_groups=mesh['rep'=16,'fsdp'=32] {'fsdp'}, dimensions={1}, use_global_device_ids=true | all-gather | bytes 16896 | tf_op jit(solution)/shard_map/all_gather | solution.py:43
  356.6 0.1 convert_reduce_fusion
  356.7 0.5 multiply_reduce_fusion
  357.2 62.4 %all-gather.2 = f32[32,1,128]{2,1,0:T(1,128)S(1)} all-gather(f32[1,1,128]{2,1,0:T(1,128)S(1)} %get-tuple-element.8), channel_id=1, replica_groups=mesh['rep'=16,'fsdp'=32] {'fsdp'}, dimensions={0}, use_global_device_ids=true | all-gather | bytes 16896 | tf_op jit(solution)/shard_map/all_gather | solution.py:30
  419.6 0.0 all-to-all-done
  419.6 0.0 copy-done.1
  419.6 0.0 copy-start.3
  419.6 4.9 %fusion.8 = f32[256]{0:T(256)} fusion(f32[4096]{0:T(1024)S(1)} %bitcast.49, bf16[256,512]{1,0:T(8,128)(2,1)S(1)} %copy-done.1, bf16[1,4096,512]{2,1,0:T(8,128)(2,1)} %all-gather.8.cloned.1.call-done, bf16[128,32,256]{0,2,1:T(8,128)(2,1)} %all-to-all-done), kind=kOutput, calls=%fused_computation.15 | convolution fusion | flops 1077935872 | bytes 6571008 | tf_op jit(solution)/shard_map/dot_general | solution.py:38
  424.5 0.0 copy-done.3
  424.5 3.7 fusion.11
  428.2 8.9 %convolution_convert_fusion = bf16[32,128,512]{2,1,0:T(8,128)(2,1)} fusion(bf16[32,256,512]{2,1,0:T(8,128)(2,1)} %bitcast.46, bf16[128,32,256]{0,2,1:T(8,128)(2,1)} %bitcast.2, f32[32,256]{1,0:T(8,128)S(1)} %reshape.53, f32[128]{0:T(128)S(1)} %get-tuple-element.9), kind=kOutput, calls=%fused_computation.10 | convolution fusion | flops 1080033280 | bytes 14713344 | tf_op jit(solution)/shard_map/tgr,grk->gtk/dot_general | solution.py:47
  437.2 3.5 reduce_sum.31
  (5 shorter events, 0.0 us)
Async XLA Ops:
  8.0 167.3 %copy-start = (bf16[1,128,8192]{2,1,0:T(8,128)(2,1)S(1)}, bf16[1,128,8192]{2,1,0:T(8,128)(2,1)}, u32[]{:S(2)}) copy-start(bf16[1,128,8192]{2,1,0:T(8,128)(2,1)} %param.11) | copy-start | bytes 6291460
  8.0 164.0 %all-reduce.2.cloned.1.call-start = ((), (), s32[]{:S(2)}) async-start(), calls=%async_computation.1 | async-start | bytes 524288 | tf_op jit(solution)/shard_map/psum | solution.py:17
  14.6 405.0 %all-gather.8.cloned.1.call-start = ((), (), s32[]{:S(2)}) async-start(), calls=%async_computation.3 | async-start | bytes 4325376 | tf_op jit(solution)/shard_map/all_gather | solution.py:32
  15.1 413.1 %all-gather.6.cloned.1.call-start = ((), (), s32[]{:S(2)}) async-start(), calls=%async_computation.2 | async-start | bytes 8650752 | tf_op jit(solution)/shard_map/all_gather | solution.py:42
  175.3 16.0 %copy-start.2 = (bf16[1,256]{1,0:T(2,128)(2,1)S(1)}, bf16[1,256]{1,0:T(2,128)(2,1)}, u32[]{:S(2)}) copy-start(bf16[1,256]{1,0:T(2,128)(2,1)} %param.12) | copy-start | bytes 1540
  177.8 241.8 %copy-start.1 = (bf16[256,512]{1,0:T(8,128)(2,1)S(1)}, bf16[256,512]{1,0:T(8,128)(2,1)}, u32[]{:S(2)}) copy-start(bf16[256,512]{1,0:T(8,128)(2,1)} %convert_element_type.57) | copy-start | bytes 786436
  177.8 241.8 %all-to-all-start = ((bf16[128,32,256]{0,2,1:T(8,128)(2,1)}), bf16[128,32,256]{0,2,1:T(8,128)(2,1)}, u32[]{:S(2)}, u32[]{:S(2)}) async-start(bf16[128,32,256]{0,2,1:T(8,128)(2,1)} %bitcast.2), calls=%async_computation | async-start | bytes 4194304 | tf_op jit(solution)/shard_map/all_to_all | solution.py:31
  419.6 5.0 %copy-start.3 = (bf16[1,4096,512]{2,1,0:T(8,128)(2,1)S(1)}, bf16[1,4096,512]{2,1,0:T(8,128)(2,1)}, u32[]{:S(2)}) copy-start(bf16[1,4096,512]{2,1,0:T(8,128)(2,1)} %all-gather.8.cloned.1.call-done) | copy-start | bytes 12582916
Sparse Core Ops, SparseCore 0:
  14.7 157.2 all-reduce.1
Sparse Core Ops, SparseCore 1:
  17.3 141.9 all-gather.7
  175.3 227.4 all-gather.5
where the time goes:
time: 448 us
  blocking collectives  228 us (51%)
  waiting for transfers between devices  157 us (35%)
  matrix products  17.6 us (4%)
  between operations  15.6 us (3%)
  starting transfers between devices  13.6 us (3%)
  other arithmetic  10.9 us (2%)
  local copies, waits for them, and re-layouts  5.4 us (1%)
    all_gather x1, blocking collectives, shards(): gain_piece = lax.all_gather(own_gain, 'fsdp', axis=0, tiled=True)  165 us
    psum x1, waiting for transfers between devices, shards(): lax.psum(decoded.astype(jnp.bfloat16), 'rep').astype(jnp.float32) / replicas  157 us
    all_gather x1, blocking collectives, shards(): every_scale = lax.all_gather(inv_rms, 'fsdp', axis=0, tiled=True)  62.4 us
    all_to_all x1, starting transfers between devices, shards(): lax.all_to_all(activations, 'fsdp', split_axis=1, concat_axis=0, tiled=True)  13.5 us
  transfers between devices with their start and end apart: 4, of which 1 were waited for; matrix products, arithmetic and copies ran while one was open for 3% of the time, Pallas kernels for 0%

commit v1 on v0

v1 whole, which is shorter than its diff:
```python
import functools

import jax
import jax.numpy as jnp
from jax import lax
from jax.experimental import pallas as pl
from jax.experimental.pallas import tpu as pltpu
from jax.sharding import PartitionSpec as P

MESH = pl.DeviceIdType.MESH
F32 = jnp.float32
BF16 = jnp.bfloat16

D = 8192
KV = 512
REP = 16
Z = 16
OWN = 256
TOK = 128
SUBS = 2
PART = OWN // SUBS
STEPS = 8
outer_rate = 0.7
momentum_decay = 0.9


def whole_wait(ref, sem):
    pltpu.make_async_copy(ref, ref, sem).wait()


def kernel(
    codes, scales, base, momentum, inputs, gain, cotangent,
    new_base, new_momentum, keys, grad_weight, grad_gain,
    decoded, pieces, averages, rows, weight, gains, halves, both, inverse,
    totals, landed, terms, key_total,
    piece_send, piece_recv, average_send, average_recv,
    half_send, half_recv, up_send, up_recv, gain_send, gain_recv,
    gain_z_send, gain_z_recv,
    sum_send, sum_recv, wz_send, wz_recv, wx_send, wx_recv, wy_send, wy1_recv, wy2_recv, wc_send, wc_recv,
):
    rep = lax.axis_index("rep")
    shard = lax.axis_index("fsdp")
    core = rep % 2
    x_hi = (rep // 2) % 2
    y = rep // 4
    x_lo = shard // Z
    z = shard % Z
    x = x_hi * 2 + x_lo

    def at(y_to=y, x_to=x, z_to=z, core_to=core):
        return ((y_to * 2 + x_to // 2) * 2 + core_to, (x_to % 2) * Z + z_to)

    up_z, down_z = at(z_to=(z + 1) % Z), at(z_to=(z + Z - 1) % Z)
    ring = (up_z, down_z)
    right, left = at(x_to=(x + 1) % 4), at(x_to=(x + 3) % 4)
    across = at(x_to=(x + 2) % 4)
    north, south = at(y_to=(y + 1) % 4), at(y_to=(y + 3) % 4)
    twin = at(core_to=1 - core)
    partner = at(x_to=x_hi * 2 + 1 - x_lo)

    def send(src, dst, send_sem, recv_sem, device):
        copy = pltpu.make_async_remote_copy(
            src_ref=src, dst_ref=dst, send_sem=send_sem, recv_sem=recv_sem,
            device_id=device, device_id_type=MESH,
        )
        copy.start()

    barrier = pltpu.get_barrier_semaphore()

    def greet(step, carry):
        pl.semaphore_signal(barrier, inc=1, device_id=((rep + step) % REP, shard), device_id_type=MESH)
        return carry

    lax.fori_loop(1, REP, greet, 0)
    for device in (up_z, down_z, right, left):
        pl.semaphore_signal(barrier, inc=1, device_id=device, device_id_type=MESH)

    entry = lax.broadcasted_iota(jnp.int32, (64, 128), 0)
    lane = lax.broadcasted_iota(jnp.int32, (64, 128), 1)
    chosen = (lane >> 1) == entry
    from_lane = lax.broadcasted_iota(jnp.int32, (128, 128), 0)
    to_lane = lax.broadcasted_iota(jnp.int32, (128, 128), 1)
    spread = ((from_lane & 1) == (to_lane >> 6)).astype(BF16)

    def decode(block, carry):
        picked = jnp.where(chosen, scales[pl.ds(block, 1), :], 0.0)
        high = picked.astype(BF16)
        low = (picked - high.astype(F32)).astype(BF16)
        scale = jnp.dot(high, spread, preferred_element_type=F32) + jnp.dot(low, spread, preferred_element_type=F32)
        code = codes[pl.ds(pl.multiple_of(block * 64, 64), 64), :]
        decoded[block] = ((code - 8).astype(F32) * scale).astype(BF16)
        return carry

    lax.fori_loop(0, REP, decode, 0)

    def squares(block, total):
        cols = inputs[:, pl.ds(pl.multiple_of(block * 512, 512), 512)].astype(F32)
        cols = cols * cols
        return total + (cols[:, :128] + cols[:, 128:256]) + (cols[:, 256:384] + cols[:, 384:])

    square = lax.fori_loop(0, D // 512, squares, jnp.zeros((TOK, 128), F32))
    inv = lax.rsqrt(jnp.sum(square, axis=1, keepdims=True) * (1.0 / D) + 1e-05)
    inverse[...] = jnp.broadcast_to(inv, (TOK, 128))
    both[0] = (cotangent[...].astype(F32) * inv).astype(BF16)
    own_gain = gain[...].astype(F32)
    gains[pl.ds(z * 2 + x_lo, 1)] = own_gain.reshape(1, 1, OWN)

    pl.semaphore_wait(barrier, REP - 1 + 4)

    def send_piece(step, carry):
        peer = (rep + step) % REP
        send(decoded.at[peer], pieces.at[step - 1], piece_send, piece_recv, (peer, shard))
        return carry

    lax.fori_loop(1, REP, send_piece, 0)

    def send_half(far):
        target = (z + far) % Z
        start = pl.multiple_of(((1 - x_lo) * Z + target) * OWN, OWN)
        send(inputs.at[:, pl.ds(start, OWN)], halves.at[target], half_send, half_recv.at[far], partner)

    order = [8]
    for far in range(7, 0, -1):
        order += [far, Z - far]
    order += [0]
    sent_halves = [0]

    def more_halves(count):
        for far in order[sent_halves[0]: sent_halves[0] + count]:
            send_half(far)
        sent_halves[0] += count

    send(both.at[0], both.at[1], up_send, up_recv, partner)
    more_halves(1)
    send(gains.at[z * 2 + x_lo], gains.at[z * 2 + x_lo], gain_send, gain_recv, partner)
    more_halves(2)

    def term(far, slot):
        target = (z + far) % Z
        whole_wait(halves.at[target], half_recv.at[far])
        start = pl.multiple_of((x_lo * Z + target) * OWN, OWN)
        cols = jnp.concatenate([inputs[:, pl.ds(start, OWN)], halves[target]], axis=0)
        terms[slot] = lax.dot_general(
            cols, both[...].reshape(2 * TOK, KV), (((0,), (0,)), ((), ())), preferred_element_type=F32
        )

    def send_sum(step, way, sub):
        part = pl.ds(sub * PART, PART)
        send(
            totals.at[way, step - 1, part], landed.at[way, step - 1, part],
            sum_send.at[way, min(step - 1, 1)], sum_recv.at[way, step - 1, sub], ring[way],
        )

    def first_way(sub):
        return 0 if sub < SUBS // 2 else 1

    def sum_unit(step, way, sub):
        part = pl.ds(sub * PART, PART)
        value = terms[way, part]
        if step > 2 or first_way(sub) == way:
            whole_wait(landed.at[way, step - 2, part], sum_recv.at[way, step - 2, sub])
            value = value + landed[way, step - 2, part].astype(F32)
        totals[way, step - 1, part] = value.astype(BF16)
        send_sum(step, way, sub)

    whole_wait(both.at[1], up_recv)
    term(8, 0)
    for sub in range(SUBS):
        way = first_way(sub)
        part = pl.ds(sub * PART, PART)
        totals[way, 0, part] = terms[0, part].astype(BF16)
        send_sum(1, way, sub)
    more_halves(2)

    whole_wait(pieces, piece_recv)

    def add_piece(step, total):
        return total + pieces[step].astype(F32)

    total = lax.fori_loop(0, REP - 1, add_piece, decoded[rep].astype(F32))
    average = (total * (1.0 / REP)).astype(BF16)
    averages[rep] = average
    average = average.astype(F32)

    def send_average(step, carry):
        send(averages.at[rep], averages.at[rep], average_send, average_recv, ((rep + step) % REP, shard))
        return carry

    own = pl.ds(pl.multiple_of(rep * 64, 64), 64)
    moved = momentum_decay * momentum[own, :] + average
    rows[...] = (base[own, :] - outer_rate * (average + momentum_decay * moved)) * D ** (-0.5)

    def block_at(z_at, core_at=core, y_at=y, x_at=x):
        return ((z_at * 2 + core_at) * 4 + y_at) * 4 + x_at

    mine = block_at(z)
    for col in range(4):
        weight[pl.ds(mine, 1), :, col * 128:(col + 1) * 128] = (
            rows[pl.ds(col, 16, stride=4), :].astype(BF16).reshape(1, 16, 128)
        )

    def send_weight_z(step):
        for way in range(2 if step < STEPS else 1):
            source = (z + Z - (step - 1)) % Z if way == 0 else (z + step - 1) % Z
            block = weight.at[block_at(source)]
            send(block, block, wz_send.at[way], wz_recv.at[way, step - 1], ring[way])
            block = gains.at[pl.ds(source * 2, 2)]
            send(block, block, gain_z_send.at[way], gain_z_recv.at[way, step - 1], ring[way])

    whole_wait(gains.at[0], gain_recv)
    send_weight_z(1)
    lax.fori_loop(1, REP, send_average, 0)

    def slices(group):
        if group in (0, STEPS):
            return ((z + group) % Z,)
        return ((z + Z - group) % Z, (z + group) % Z)

    def arrived_z(group):
        for way in range(2 if group < STEPS else 1):
            whole_wait(weight.at[0], wz_recv.at[way, group - 1])
            whole_wait(gains.at[pl.ds(0, 2)], gain_z_recv.at[way, group - 1])

    def send_x(group):
        for at_z in slices(group):
            block = weight.at[block_at(at_z)]
            for device in (right, left, across):
                send(block, block, wx_send, wx_recv.at[group], device)

    def send_y1(group):
        held = slices(group)
        whole_wait(weight.at[pl.ds(0, 3 * len(held))], wx_recv.at[group])
        for at_z in held:
            block = weight.at[pl.ds(block_at(at_z, x_at=0), 4)]
            for device in (north, south):
                send(block, block, wy_send, wy1_recv.at[group], device)

    def send_y2(group):
        held = slices(group)
        whole_wait(weight.at[pl.ds(0, 8 * len(held))], wy1_recv.at[group])
        for way, at_z in enumerate(held):
            y_from = (y + 3) % 4 if way == 0 else (y + 1) % 4
            block = weight.at[pl.ds(block_at(at_z, y_at=y_from, x_at=0), 4)]
            send(block, block, wy_send, wy2_recv.at[group], (north, south)[way])

    def send_core(group):
        held = slices(group)
        whole_wait(weight.at[pl.ds(0, 4 * len(held))], wy2_recv.at[group])
        for at_z in held:
            block = weight.at[pl.ds(block_at(at_z, y_at=0, x_at=0), 16)]
            send(block, block, wc_send, wc_recv.at[group], twin)

    def project(group):
        held = slices(group)
        whole_wait(weight.at[pl.ds(0, 16 * len(held))], wc_recv.at[group])
        for at_z in held:
            def one(lo, carry):
                start = pl.multiple_of((lo * Z + at_z) * OWN, OWN)
                scale = jnp.concatenate([inverse[...]] * 2, axis=1)
                normed = inputs[:, pl.ds(start, OWN)].astype(F32) * scale * gains[at_z * 2 + lo]
                parts = [
                    weight[block_at(at_z, member % 2, member // 4, ((member // 2) % 2) * 2 + lo)]
                    for member in range(REP)
                ]
                value = jnp.dot(
                    normed.astype(BF16), jnp.concatenate(parts, axis=0), preferred_element_type=F32
                )
                key_total[...] += value.astype(BF16).astype(F32)
                return carry

            lax.fori_loop(0, 2, one, 0)

    def outer_step():
        whole_wait(averages.at[pl.ds(0, REP - 1)], average_recv)

        def one(block, carry):
            at_rows = pl.ds(pl.multiple_of(block * 64, 64), 64)
            average = averages[block].astype(F32)
            moved = momentum_decay * momentum[at_rows, :] + average
            new_momentum[at_rows, :] = moved
            new_base[at_rows, :] = base[at_rows, :] - outer_rate * (average + momentum_decay * moved)
            return carry

        lax.fori_loop(0, REP, one, 0)

    key_total[...] = jnp.zeros_like(key_total)
    send_x(0)

    stages = (send_y1, send_y2, send_core, project)

    def weight_slot(slot):
        if 1 <= slot <= STEPS:
            arrived_z(slot)
            if slot < STEPS:
                send_weight_z(slot + 1)
            send_x(slot)
        for behind, stage in enumerate(stages):
            group = slot - 1 - behind
            if 0 <= group <= STEPS:
                stage(group)

    slot = 1
    for step in range(2, STEPS + 1):
        term(9 - step, 0)
        term(Z - (9 - step), 1)
        more_halves(3)
        for sub in range(SUBS):
            for way in range(2):
                sum_unit(step, way, sub)
            weight_slot(slot)
            slot += 1
            if slot == 4:
                outer_step()
    while slot - 1 - len(stages) < STEPS:
        weight_slot(slot)
        slot += 1
    keys[...] = key_total[...].astype(BF16)

    term(0, 0)
    gain_col = jnp.transpose(jnp.broadcast_to(own_gain, (128, OWN)))
    dots = jnp.zeros((OWN, 128), F32)
    for sub in range(SUBS):
        for way in range(2):
            part = pl.ds(sub * PART, PART)
            whole_wait(landed.at[way, STEPS - 1, part], sum_recv.at[way, STEPS - 1, sub])
    for col in range(4):
        cols = slice(col * 128, (col + 1) * 128)
        value = (
            terms[0, :, cols] + landed[0, STEPS - 1, :, cols].astype(F32) + landed[1, STEPS - 1, :, cols].astype(F32)
        )
        grad_weight[:, cols] = value * gain_col
        row = (new_base[pl.ds(col, OWN, stride=4), :] * D ** (-0.5)).astype(BF16).astype(F32)
        dots = dots + row * value
    grad_gain[...] = jnp.sum(jnp.transpose(dots), axis=0, keepdims=True)

    whole_wait(pieces, piece_send)
    whole_wait(averages.at[pl.ds(0, REP - 1)], average_send)
    whole_wait(halves, half_send)
    whole_wait(both.at[1], up_send)
    whole_wait(gains.at[0], gain_send)
    for way in range(2):
        whole_wait(totals.at[way, 0, pl.ds(0, OWN // 2)], sum_send.at[way, 0])
        whole_wait(totals.at[way, pl.ds(1, STEPS - 1)], sum_send.at[way, 1])
        count = STEPS - way
        whole_wait(weight.at[pl.ds(0, count)], wz_send.at[way])
        whole_wait(gains.at[pl.ds(0, 2 * count)], gain_z_send.at[way])
    whole_wait(weight.at[pl.ds(0, 3 * Z)], wx_send)
    whole_wait(weight.at[pl.ds(0, 12 * Z)], wy_send)
    whole_wait(weight.at[pl.ds(0, 16 * Z)], wc_send)


def shards(codes, scales, base, momentum, inputs, gain, cotangent):
    vmem = pl.BlockSpec(memory_space=pltpu.VMEM)
    dma = pltpu.SemaphoreType.DMA
    out = pl.pallas_call(
        kernel,
        out_shape=(
            jax.ShapeDtypeStruct((1024, 128), F32),
            jax.ShapeDtypeStruct((1024, 128), F32),
            jax.ShapeDtypeStruct((TOK, KV), BF16),
            jax.ShapeDtypeStruct((OWN, KV), F32),
            jax.ShapeDtypeStruct((1, OWN), F32),
        ),
        in_specs=[vmem] * 7,
        out_specs=[vmem] * 5,
        scratch_shapes=[
            pltpu.VMEM((REP, 64, 128), BF16),
            pltpu.VMEM((REP - 1, 64, 128), BF16),
            pltpu.VMEM((REP, 64, 128), BF16),
            pltpu.VMEM((64, 128), F32),
            pltpu.VMEM((512, 16, KV), BF16),
            pltpu.VMEM((2 * Z, 1, OWN), F32),
            pltpu.VMEM((Z, TOK, OWN), BF16),
            pltpu.VMEM((2, TOK, KV), BF16),
            pltpu.VMEM((TOK, 128), F32),
            pltpu.VMEM((2, STEPS, OWN, KV), BF16),
            pltpu.VMEM((2, STEPS, OWN, KV), BF16),
            pltpu.VMEM((2, OWN, KV), F32),
            pltpu.VMEM((TOK, KV), F32),
            dma, dma, dma, dma,
            dma, dma((Z,)), dma, dma, dma, dma,
            dma((2,)), dma((2, STEPS)),
            dma((2, 2)), dma((2, STEPS, SUBS)), dma((2,)), dma((2, STEPS)),
            dma, dma((STEPS + 1,)), dma, dma((STEPS + 1,)), dma((STEPS + 1,)), dma, dma((STEPS + 1,)),
        ],
        compiler_params=pltpu.CompilerParams(
            collective_id=0, has_side_effects=True, vmem_limit_bytes=56 * 1024 * 1024
        ),
    )(
        codes.reshape(1024, 128), scales.reshape(16, 128), base.reshape(1024, 128), momentum.reshape(1024, 128),
        inputs[0], gain, cotangent[0],
    )
    new_base, new_momentum, keys, grad_weight, grad_gain = out
    return new_base.reshape(-1), new_momentum.reshape(-1), keys[None], grad_weight[None], grad_gain


def solution(mesh):
    placed = (
        P("rep", "fsdp"),
        P("rep", "fsdp"),
        P("fsdp"),
        P("fsdp"),
        P("rep", "fsdp", None),
        P("rep", "fsdp"),
        P("rep", "fsdp", None),
    )
    return jax.shard_map(
        shards,
        mesh=mesh,
        in_specs=placed,
        out_specs=(
            P("fsdp"),
            P("fsdp"),
            P("rep", "fsdp", None),
            P("rep", "fsdp", None),
            P("rep", "fsdp"),
        ),
        check_vma=False,
    )
```

time: 448 us -> 101 us (0.23)
  the two profiles are of different devices: /device:TPU:32 before, /device:TPU:1 now
where the time goes in v1:
time: 101 us
  Pallas kernels  94.6 us (94%)
  local copies, waits for them, and re-layouts  5.82 us (6%)
    pallas_call x1, Pallas kernels, shards(): pl.pallas_call(kernel, out_shape=(jax.ShapeDtypeStruct((1024, 128), F32),...  94.6 us
    unnamed x11, local copies, waits for them, and re-layouts  5.82 us

profile of v1, /device:TPU:1, one launch (start us, length us, event | category | flops | bytes accessed | tf_op | source)
XLA Modules:
  0.0 101.1 jit_solution(371654759031503178)
XLA Ops:
  0.6 94.6 %shard_map.110 = (f32[1024,128]{1,0:T(8,128)}, f32[1024,128]{1,0:T(8,128)}, bf16[128,512]{1,0:T(8,128)(2,1)}, f32[256,512]{1,0:T(8,128)}, f32[1,256]{1,0:T(1,128)}) custom-call(s32[1024,128]{1,0:T(8,128)} %bitcast.14, f32[16,128]{1,0:T(8,128)} %bitcast.19, f32[1024,128]{1,0:T(8,128)} %bitcast.15, f32[1024,128]{1,0:T(8,128)} %bitcast.16, ...), custom_call_target="tpu_custom_call" | custom-call | tf_op jit(solution)/shard_map/pallas_call | solution.py:355
  95.3 0.0 copy-start.1
  95.3 0.0 copy-start
  95.3 0.0 copy-start.2
  95.3 1.9 %copy.17 = f32[131072]{0:T(1024)} copy(f32[131072]{0:T(1024)} %bitcast.13) | data formatting | bytes 1048576
  97.2 1.9 %copy.18 = f32[131072]{0:T(1024)} copy(f32[131072]{0:T(1024)} %bitcast.12) | data formatting | bytes 1048576
  99.1 0.0 copy-done.1
  99.1 0.7 copy.19
  99.7 0.0 copy-done
  99.7 0.8 copy.20
  100.5 0.0 copy-done.2
  100.5 0.6 copy.21
Async XLA Ops:
  95.3 3.8 %copy-start.1 = (bf16[128,512]{1,0:T(8,128)(2,1)S(1)}, bf16[128,512]{1,0:T(8,128)(2,1)}, u32[]{:S(2)}) copy-start(bf16[128,512]{1,0:T(8,128)(2,1)} %get-tuple-element.12) | copy-start | bytes 393220
  95.3 4.5 %copy-start = (f32[256,512]{1,0:T(8,128)S(1)}, f32[256,512]{1,0:T(8,128)}, u32[]{:S(2)}) copy-start(f32[256,512]{1,0:T(8,128)} %get-tuple-element.13) | copy-start | bytes 1572868
  95.3 5.3 %copy-start.2 = (f32[1,256]{1,0:T(1,128)S(1)}, f32[1,256]{1,0:T(1,128)}, u32[]{:S(2)}) copy-start(f32[1,256]{1,0:T(1,128)} %get-tuple-element.24) | copy-start | bytes 3076

commit v2 on v0

v2 whole, which is shorter than its diff:
```python
import jax
import jax.numpy as jnp
from jax import lax
from jax.experimental import pallas as pl
from jax.experimental.pallas import tpu as pltpu
from jax.sharding import PartitionSpec as P

MESH = pl.DeviceIdType.MESH
F32 = jnp.float32
BF16 = jnp.bfloat16

D = 8192
KV = 512
Z = 16
OWN = 256
TOK = 128
SUBS = 4
PART = KV // SUBS
STEPS = 8
outer_rate = 0.7
momentum_decay = 0.9

HOPS = (
    ((0, 5), (0, 11)),
    ((0, 1), (0, 15), (5, 1), (5, 15), (-5, 1), (-5, 15), (-5, 3)),
    ((-1, 1), (4, 1), (-6, 1), (1, 15), (-4, 15), (6, 15)),
)
GROUPS = ((0,), (5, -5), (1, -1, 4, -4, 6, -6, 8), (2, -2, 3, -3, 7, -7))
Y_FIRST = (6, -6, 8, 7, -7, 3)


def whole_wait(ref, sem):
    pltpu.make_async_copy(ref, ref, sem).wait()


def kernel(
    codes_hbm, scales_hbm, base_hbm, momentum_hbm, inputs_hbm, gain, cotangent_hbm,
    base_out, momentum_out, keys_out, weight_out, gain_out,
    codes, scales, base, momentum, inputs, cotangent, new_base, new_momentum, keys, grad_weight,
    decoded, twin_part, pairs, pieces, averages, rows, weight, gains, halves, both, inverse,
    normed, twin_normed, totals, landed, terms, key_total, key_twin,
    local_sem, out_sem, twin_send, twin_recv, piece_send, piece_recv,
    average_send, average_recv, average_twin_send, average_twin_recv,
    half_send, half_recv, up_send, up_recv, gain_send, gain_recv, gain_z_send, gain_z_recv,
    normed_send, normed_recv, key_send, key_recv, sum_send, sum_recv, wz_send, wz_recv,
    first_send, first_recv, second_send, second_recv, third_recv,
):
    rep = lax.axis_index("rep")
    shard = lax.axis_index("fsdp")
    core = rep % 2
    x_hi = (rep // 2) % 2
    y = rep // 4
    x_lo = shard // Z
    z = shard % Z
    x = x_hi * 2 + x_lo
    chip = rep // 2
    own = core * 8 + chip

    def at(y_to=y, x_to=x, z_to=z, core_to=core):
        return ((y_to * 2 + x_to // 2) * 2 + core_to, (x_to % 2) * Z + z_to)

    def along_z(by):
        return at(z_to=(z + by) % Z)

    def fellow(step):
        return ((chip + step) % 8) * 2 + core, shard

    ring = (along_z(1), along_z(15))
    right, left, across = (at(x_to=(x + by) % 4) for by in (1, 3, 2))
    north, south, over = (at(y_to=(y + by) % 4) for by in (1, 3, 2))
    twin = at(core_to=1 - core)
    partner = at(x_to=x_hi * 2 + 1 - x_lo)

    def send(src, dst, send_sem, recv_sem, device):
        pltpu.make_async_remote_copy(
            src_ref=src, dst_ref=dst, send_sem=send_sem, recv_sem=recv_sem,
            device_id=device, device_id_type=MESH,
        ).start()

    barrier = pltpu.get_barrier_semaphore()

    def greet(step, carry):
        pl.semaphore_signal(barrier, inc=1, device_id=fellow(step), device_id_type=MESH)
        return carry

    lax.fori_loop(1, 8, greet, 0)
    near = [twin, right, left] + [along_z(by) for by in (1, 15, 5, 11, 3, 13)]
    for device in near:
        pl.semaphore_signal(barrier, inc=1, device_id=device, device_id_type=MESH)

    def load(src, dst, index):
        pltpu.make_async_copy(src, dst, local_sem.at[index]).start()

    load(codes_hbm, codes, 5)
    load(scales_hbm, scales, 6)
    quarter = D // 4
    for index in range(4):
        cols = pl.ds(index * quarter, quarter)
        load(inputs_hbm.at[:, cols], inputs.at[:, cols], index)
    load(cotangent_hbm, cotangent, 4)
    load(base_hbm, base, 7)
    load(momentum_hbm, momentum, 8)

    entry = lax.broadcasted_iota(jnp.int32, (64, 128), 0)
    lane = lax.broadcasted_iota(jnp.int32, (64, 128), 1)
    chosen = (lane >> 1) == entry
    from_lane = lax.broadcasted_iota(jnp.int32, (128, 128), 0)
    to_lane = lax.broadcasted_iota(jnp.int32, (128, 128), 1)
    spread = ((from_lane & 1) == (to_lane >> 6)).astype(BF16)

    def decode(block, carry):
        picked = jnp.where(chosen, scales[pl.ds(block, 1), :], 0.0)
        high = picked.astype(BF16)
        low = (picked - high.astype(F32)).astype(BF16)
        scale = jnp.dot(high, spread, preferred_element_type=F32) + jnp.dot(low, spread, preferred_element_type=F32)
        code = codes[pl.ds(pl.multiple_of(block * 64, 64), 64), :]
        decoded[block] = ((code - 8).astype(F32) * scale).astype(BF16)
        return carry

    whole_wait(codes, local_sem.at[5])
    whole_wait(scales, local_sem.at[6])
    lax.fori_loop(0, 16, decode, 0)

    def squares(block, total):
        cols = inputs[:, pl.ds(pl.multiple_of(block * 512, 512), 512)].astype(F32)
        cols = cols * cols
        return total + (cols[:, :128] + cols[:, 128:256]) + (cols[:, 256:384] + cols[:, 384:])

    square = jnp.zeros((TOK, 128), F32)
    for index in range(4):
        cols = inputs.at[:, pl.ds(index * quarter, quarter)]
        whole_wait(cols, local_sem.at[index])
        square = lax.fori_loop(index * 4, index * 4 + 4, squares, square)
    inv = lax.rsqrt(jnp.sum(square, axis=1, keepdims=True) * (1.0 / D) + 1e-05)
    inverse[...] = jnp.broadcast_to(inv, (TOK, 128))
    whole_wait(cotangent, local_sem.at[4])
    for sub in range(SUBS):
        both[sub, 0] = (cotangent[:, sub * PART:(sub + 1) * PART].astype(F32) * inv).astype(BF16)
    own_gain = gain[...].astype(F32)
    gains[pl.ds(z * 2 + x_lo, 1)] = own_gain.reshape(1, 1, OWN)

    pl.semaphore_wait(barrier, 7 + len(near))

    def send_half(far):
        target = (z + far) % Z
        start = pl.multiple_of(((1 - x_lo) * Z + target) * OWN, OWN)
        send(inputs.at[:, pl.ds(start, OWN)], halves.at[target], half_send, half_recv.at[far], partner)

    def send_up(sub):
        send(both.at[sub, 0], both.at[sub, 1], up_send, up_recv.at[sub], partner)

    send(decoded.at[pl.ds((1 - core) * 8, 8)], twin_part, twin_send, twin_recv, twin)
    send(gains.at[z * 2 + x_lo], gains.at[z * 2 + x_lo], gain_send, gain_recv, partner)
    send_up(0)
    send_half(8)
    for sub in (2, 1, 3):
        send_up(sub)
    send_half(7)
    send_half(9)

    whole_wait(twin_part, twin_recv)
    for block in range(8):
        pairs[block] = (decoded[core * 8 + block].astype(F32) + twin_part[block].astype(F32)).astype(BF16)

    def send_piece(step, carry):
        send(pairs.at[(chip + step) % 8], pieces.at[step - 1], piece_send, piece_recv, fellow(step))
        return carry

    lax.fori_loop(1, 8, send_piece, 0)

    def features(far):
        target = (z + far) % Z
        whole_wait(halves.at[target], half_recv.at[far])
        start = pl.multiple_of((x_lo * Z + target) * OWN, OWN)
        return jnp.concatenate([inputs[:, pl.ds(start, OWN)], halves[target]], axis=0)

    def product(cols, cotangents):
        return lax.dot_general(cols, cotangents, (((0,), (0,)), ((), ())), preferred_element_type=F32)

    def term(far, slot):
        cotangents = jnp.concatenate([both[sub].reshape(2 * TOK, PART) for sub in range(SUBS)], axis=1)
        terms[slot] = product(features(far), cotangents)

    def send_sum(step, way, sub, value):
        totals[way, step - 1, sub] = value.astype(BF16)
        send(
            totals.at[way, step - 1, sub], landed.at[way, step - 1, sub],
            sum_send.at[way, min(step - 1, 1)], sum_recv.at[way, step - 1, sub], ring[way],
        )

    def sum_unit(step, way, sub, fresh=False):
        value = terms[way, :, sub * PART:(sub + 1) * PART]
        if not fresh:
            whole_wait(landed.at[way, step - 2, sub], sum_recv.at[way, step - 2, sub])
            value = value + landed[way, step - 2, sub].astype(F32)
        send_sum(step, way, sub, value)

    cols = features(8)
    for sub in (0, 2, 1, 3):
        whole_wait(both.at[sub, 1], up_recv.at[sub])
        send_sum(1, sub // 2, sub, product(cols, both[sub].reshape(2 * TOK, PART)))
    send_half(6)
    send_half(10)

    def gain_event(level):
        if level == 0:
            whole_wait(gains.at[0], gain_recv)
        else:
            whole_wait(gains.at[pl.ds(0, 2 * len(GROUPS[level]))], gain_z_recv.at[level - 1])
        if level < 3:
            for far, by in HOPS[level]:
                block = gains.at[pl.ds(((z + far + Z) % Z) * 2, 2)]
                send(block, block, gain_z_send, gain_z_recv.at[level], along_z(by))

    gain_event(0)
    term(7, 0)
    term(9, 1)
    for sub in (2, 0, 3, 1):
        sum_unit(2, 1 - sub // 2, sub, fresh=True)
    send_half(5)
    send_half(11)
    for sub in (0, 2, 1, 3):
        sum_unit(2, sub // 2, sub)

    mine = pl.ds(pl.multiple_of(own * 64, 64), 64)

    def slice_at(far):
        return (z + far + Z) % Z

    def start_weight():
        whole_wait(pieces, piece_recv)
        total = pairs[chip].astype(F32)
        for step in range(7):
            total = total + pieces[step].astype(F32)
        average = (total * (1.0 / 16)).astype(BF16)
        averages[own] = average
        average = average.astype(F32)
        whole_wait(base, local_sem.at[7])
        whole_wait(momentum, local_sem.at[8])
        moved = momentum_decay * momentum[mine, :] + average
        rows[...] = (base[mine, :] - outer_rate * (average + momentum_decay * moved)) * D ** (-0.5)
        for col in range(4):
            weight[z, y, x, :, col * 128:(col + 1) * 128] = rows[pl.ds(col, 16, stride=4), :].astype(BF16)
        send_z(0)
        send_first(0)

    def send_averages():
        def one(step, carry):
            send(averages.at[own], averages.at[own], average_send, average_recv, fellow(step))
            return carry

        lax.fori_loop(1, 8, one, 0)

    def swap_averages():
        whole_wait(averages.at[pl.ds(0, 7)], average_recv)
        block = averages.at[pl.ds(core * 8, 8)]
        send(block, block, average_twin_send, average_twin_recv, twin)

    def outer_step():
        whole_wait(averages.at[pl.ds(0, 8)], average_twin_recv)

        def one(block, carry):
            at_rows = pl.ds(pl.multiple_of(block * 64, 64), 64)
            average = averages[block].astype(F32)
            moved = momentum_decay * momentum[at_rows, :] + average
            new_momentum[at_rows, :] = moved
            new_base[at_rows, :] = base[at_rows, :] - outer_rate * (average + momentum_decay * moved)
            return carry

        lax.fori_loop(0, 16, one, 0)
        pltpu.make_async_copy(new_base, base_out, out_sem.at[0]).start()
        pltpu.make_async_copy(new_momentum, momentum_out, out_sem.at[1]).start()

    def send_z(level):
        for far, by in HOPS[level]:
            block = weight.at[slice_at(far), y, x]
            send(block, block, wz_send, wz_recv.at[level], along_z(by))

    def z_event(level):
        whole_wait(weight.at[pl.ds(0, len(GROUPS[level + 1])), 0, 0], wz_recv.at[level])
        if level < 2:
            send_z(level + 1)
        send_first(level + 1)

    def send_first(group):
        for far in GROUPS[group]:
            block = weight.at[slice_at(far), y, x]
            for device in (north, south, over) if far in Y_FIRST else (right, left, across):
                send(block, block, first_send, first_recv.at[group], device)

    def send_second(group):
        whole_wait(weight.at[pl.ds(0, len(GROUPS[group])), 0, pl.ds(0, 3)], first_recv.at[group])
        for far in GROUPS[group]:
            held = weight.at[slice_at(far)]
            if far in Y_FIRST:
                block, devices = held.at[:, x], (right, left)
            else:
                block, devices = held.at[y], (north, south)
            for device in devices:
                send(block, block, second_send, second_recv.at[group], device)

    def send_third(group):
        whole_wait(weight.at[pl.ds(0, len(GROUPS[group])), pl.ds(0, 2)], second_recv.at[group])
        turns = [0, 0]
        for far in GROUPS[group]:
            held = weight.at[slice_at(far)]
            kind = int(far in Y_FIRST)
            way = turns[kind] % 2
            turns[kind] += 1
            if kind:
                block, device = held.at[:, (x + 3 - 2 * way) % 4], (right, left)[way]
            else:
                block, device = held.at[(y + 3 - 2 * way) % 4], (north, south)[way]
            send(block, block, second_send, third_recv.at[group], device)

    def normalize(part):
        def one(block, carry):
            start = pl.multiple_of(block * OWN, OWN)
            scale = jnp.concatenate([inverse[...]] * 2, axis=1)
            feature = (block % Z) * 2 + block // Z
            value = (inputs[:, pl.ds(start, OWN)].astype(F32) * scale * gains[feature]).astype(BF16)
            normed[0, block] = value[:, :128]
            normed[1, block] = value[:, 128:]
            return carry

        lax.fori_loop(part * 8, part * 8 + 8, one, 0)
        blocks = pl.ds(part * 8, 8)
        send(normed.at[1 - core, blocks], twin_normed.at[blocks], normed_send, normed_recv, twin)

    def project(group, first=0, last=None):
        if group == 0:
            whole_wait(twin_normed, normed_recv)
        if first == 0:
            whole_wait(weight.at[pl.ds(0, len(GROUPS[group])), 0], third_recv.at[group])
        total = key_total[...]
        for far in GROUPS[group][first:last]:
            at_z = slice_at(far)
            cols = jnp.concatenate([
                jnp.concatenate([held[lo * Z + at_z] for lo in range(2)], axis=1)
                for held in (normed.at[core], twin_normed)
            ], axis=0)
            parts = [
                weight[at_z, member // 2, (member % 2) * 2 + lo] for lo in range(2) for member in range(8)
            ]
            total = total + jnp.dot(cols, jnp.concatenate(parts, axis=0), preferred_element_type=F32)
        key_total[...] = total

    def send_keys():
        send(key_total.at[pl.ds(TOK, TOK)], key_twin, key_send, key_recv, twin)

    key_total[...] = jnp.zeros_like(key_total)
    plan = {
        (2, 3): ((start_weight,), (gain_event, 1)),
        (3, 1): ((z_event, 0), (gain_event, 2)),
        (3, 2): ((send_second, 0), (send_averages,)),
        (4, 0): ((z_event, 1), (send_second, 1)),
        (4, 1): ((send_third, 0), (gain_event, 3)),
        (4, 2): ((normalize, 0),),
        (4, 3): ((z_event, 2), (send_third, 1)),
        (5, 0): ((send_second, 2),),
        (5, 1): ((normalize, 1), (swap_averages,)),
        (5, 2): ((normalize, 2),),
        (5, 3): ((send_second, 3),),
        (6, 0): ((normalize, 3),),
        (6, 1): ((outer_step,),),
        (6, 2): ((send_third, 2),),
        (6, 3): ((project, 0),),
        (7, 0): ((project, 1),),
        (7, 1): ((send_third, 3),),
        (7, 2): ((project, 2, 0, 4),),
        (7, 3): ((project, 2, 4),),
        (8, 1): ((project, 3, 0, 3),),
        (8, 2): ((project, 3, 3), (send_keys,)),
    }
    for step in range(2, STEPS + 1):
        if step > 2:
            term(9 - step, 0)
            term(Z - (9 - step), 1)
            if step < 8:
                send_half(7 - step)
                if step < 7:
                    send_half(9 + step)
        for sub in range(SUBS):
            if step > 2:
                sum_unit(step, 0, (sub + SUBS // 2) % SUBS)
                sum_unit(step, 1, sub)
            for call, *args in plan.get((step, sub), ()):
                call(*args)

    term(0, 0)
    gain_col = jnp.transpose(jnp.broadcast_to(own_gain, (128, OWN)))
    dots = jnp.zeros((OWN, 128), F32)
    whole_wait(key_twin, key_recv)
    keys[...] = (key_total[:TOK] + key_twin[...]).astype(BF16)
    pltpu.make_async_copy(keys, keys_out, out_sem.at[2]).start()
    for sub in range(SUBS):
        cols = slice(sub * PART, (sub + 1) * PART)
        value = terms[0, :, cols]
        for way in range(2):
            whole_wait(landed.at[way, STEPS - 1, sub], sum_recv.at[way, STEPS - 1, sub])
            value = value + landed[way, STEPS - 1, sub].astype(F32)
        grad_weight[:, cols] = value * gain_col
        row = (new_base[pl.ds(sub, OWN, stride=4), :] * D ** (-0.5)).astype(BF16).astype(F32)
        dots = dots + row * value
    pltpu.make_async_copy(grad_weight, weight_out, out_sem.at[3]).start()
    gain_out[...] = jnp.sum(jnp.transpose(dots), axis=0, keepdims=True)

    whole_wait(twin_part, twin_send)
    whole_wait(pieces, piece_send)
    whole_wait(averages.at[pl.ds(0, 7)], average_send)
    whole_wait(averages.at[pl.ds(0, 8)], average_twin_send)
    whole_wait(halves, half_send)
    whole_wait(both.at[:, 1], up_send)
    whole_wait(gains.at[0], gain_send)
    whole_wait(gains.at[pl.ds(0, 30)], gain_z_send)
    whole_wait(twin_normed, normed_send)
    whole_wait(key_twin, key_send)
    for way in range(2):
        whole_wait(totals.at[way, 0, pl.ds(0, SUBS // 2)], sum_send.at[way, 0])
        whole_wait(totals.at[way, pl.ds(1, STEPS - 1)], sum_send.at[way, 1])
    whole_wait(weight.at[pl.ds(0, 15), 0, 0], wz_send)
    whole_wait(weight.at[pl.ds(0, 3)], first_send)
    whole_wait(weight.at[pl.ds(0, 12)], second_send)
    for index, (src, dst) in enumerate((
        (new_base, base_out), (new_momentum, momentum_out), (keys, keys_out), (grad_weight, weight_out),
    )):
        pltpu.make_async_copy(src, dst, out_sem.at[index]).wait()


def finish(*refs):
    count = len(refs) // 2
    sem = refs[-1]
    for index in range(count):
        pltpu.make_async_copy(refs[index], refs[count + index], sem.at[index]).start()
    for index in range(count):
        pltpu.make_async_copy(refs[index], refs[count + index], sem.at[index]).wait()


def shards(codes, scales, base, momentum, inputs, gain, cotangent):
    vmem = pl.BlockSpec(memory_space=pltpu.VMEM)
    hbm = pl.BlockSpec(memory_space=pl.ANY)
    dma = pltpu.SemaphoreType.DMA
    results = (
        jax.ShapeDtypeStruct((1024, 128), F32),
        jax.ShapeDtypeStruct((1024, 128), F32),
        jax.ShapeDtypeStruct((TOK, KV), BF16),
        jax.ShapeDtypeStruct((OWN, KV), F32),
        jax.ShapeDtypeStruct((1, OWN), F32),
    )
    out = pl.pallas_call(
        kernel,
        out_shape=results,
        in_specs=[hbm] * 5 + [vmem, hbm],
        out_specs=[hbm] * 4 + [vmem],
        scratch_shapes=[
            pltpu.VMEM((1024, 128), jnp.int32),
            pltpu.VMEM((16, 128), F32),
            pltpu.VMEM((1024, 128), F32),
            pltpu.VMEM((1024, 128), F32),
            pltpu.VMEM((TOK, D), BF16),
            pltpu.VMEM((TOK, KV), BF16),
            pltpu.VMEM((1024, 128), F32),
            pltpu.VMEM((1024, 128), F32),
            pltpu.VMEM((TOK, KV), BF16),
            pltpu.VMEM((OWN, KV), F32),
            pltpu.VMEM((16, 64, 128), BF16),
            pltpu.VMEM((8, 64, 128), BF16),
            pltpu.VMEM((8, 64, 128), BF16),
            pltpu.VMEM((7, 64, 128), BF16),
            pltpu.VMEM((16, 64, 128), BF16),
            pltpu.VMEM((64, 128), F32),
            pltpu.VMEM((Z, 4, 4, 16, KV), BF16),
            pltpu.VMEM((2 * Z, 1, OWN), F32),
            pltpu.VMEM((Z, TOK, OWN), BF16),
            pltpu.VMEM((SUBS, 2, TOK, PART), BF16),
            pltpu.VMEM((TOK, 128), F32),
            pltpu.VMEM((2, 2 * Z, TOK, 128), BF16),
            pltpu.VMEM((2 * Z, TOK, 128), BF16),
            pltpu.VMEM((2, STEPS, SUBS, OWN, PART), BF16),
            pltpu.VMEM((2, STEPS, SUBS, OWN, PART), BF16),
            pltpu.VMEM((2, OWN, KV), F32),
            pltpu.VMEM((2 * TOK, KV), F32),
            pltpu.VMEM((TOK, KV), F32),
            dma((9,)), dma((4,)), dma, dma, dma, dma,
            dma, dma, dma, dma,
            dma, dma((Z,)), dma, dma((SUBS,)), dma, dma, dma, dma((3,)),
            dma, dma, dma, dma, dma((2, 2)), dma((2, STEPS, SUBS)), dma, dma((3,)),
            dma, dma((4,)), dma, dma((4,)), dma((4,)),
        ],
        compiler_params=pltpu.CompilerParams(
            collective_id=0, has_side_effects=True, vmem_limit_bytes=58 * 1024 * 1024
        ),
    )(
        codes.reshape(1024, 128), scales.reshape(16, 128), base.reshape(1024, 128), momentum.reshape(1024, 128),
        inputs[0], gain, cotangent[0],
    )
    out = pl.pallas_call(
        finish, out_shape=results, in_specs=[vmem] * 5, out_specs=[hbm] * 5, scratch_shapes=[dma((5,))],
    )(*out)
    new_base, new_momentum, keys, grad_weight, grad_gain = out
    return new_base.reshape(-1), new_momentum.reshape(-1), keys[None], grad_weight[None], grad_gain


def solution(mesh):
    placed = (
        P("rep", "fsdp"),
        P("rep", "fsdp"),
        P("fsdp"),
        P("fsdp"),
        P("rep", "fsdp", None),
        P("rep", "fsdp"),
        P("rep", "fsdp", None),
    )
    return jax.shard_map(
        shards,
        mesh=mesh,
        in_specs=placed,
        out_specs=(
            P("fsdp"),
            P("fsdp"),
            P("rep", "fsdp", None),
            P("rep", "fsdp", None),
            P("rep", "fsdp"),
        ),
        check_vma=False,
    )
```

time: 448 us -> 80.6 us (0.18)
  the two profiles are of different devices: /device:TPU:32 before, /device:TPU:4 now
where the time goes in v2:
time: 80.6 us; the launch traced here: 80.4 us
  Pallas kernels  79.8 us (99%)
    pallas_call x1, Pallas kernels, shards(): pl.pallas_call(kernel, out_shape=results, in_specs=[hbm] * 5 + [vmem, hbm...  77.2 us
    pallas_call x1, Pallas kernels, shards(): pl.pallas_call(finish, out_shape=results, in_specs=[vmem] * 5, out_specs=...  2.61 us

profile of v2, /device:TPU:4, one launch (start us, length us, event | category | flops | bytes accessed | tf_op | source)
XLA Modules:
  0.0 80.4 jit_solution(7753931455969023032)
XLA Ops:
  0.6 77.2 %shard_map.110 = (f32[1024,128]{1,0:T(8,128)}, f32[1024,128]{1,0:T(8,128)}, bf16[128,512]{1,0:T(8,128)(2,1)}, f32[256,512]{1,0:T(8,128)}, f32[1,256]{1,0:T(1,128)}) custom-call(s32[1024,128]{1,0:T(8,128)} %bitcast.11, f32[16,128]{1,0:T(8,128)} %bitcast.15, f32[1024,128]{1,0:T(8,128)} %bitcast.12, f32[1024,128]{1,0:T(8,128)} %bitcast.13, ...), custom_call_target="tpu_custom_call" | custom-call | tf_op jit(solution)/shard_map/pallas_call | solution.py:450
  77.8 2.6 %shard_map.111 = (f32[1024,128]{1,0:T(8,128)}, f32[1024,128]{1,0:T(8,128)}, bf16[128,512]{1,0:T(8,128)(2,1)}, f32[256,512]{1,0:T(8,128)}, f32[1,256]{1,0:T(1,128)}) custom-call(f32[1024,128]{1,0:T(8,128)} %get-tuple-element.15.refs_0_, f32[1024,128]{1,0:T(8,128)} %get-tuple-element.16.refs_1_, bf16[128,512]{1,0:T(8,128)(2,1)} %get-tuple-element.17.refs_2_, ...), custom_call_target="tpu_custom_call" | custom-call | tf_op jit(solution)/shard_map/pallas_call | solution.py:497

commit v3 on v2

--- a/solution.py
+++ b/solution.py
@@ -21,12 +21,16 @@
 momentum_decay = 0.9
 
 HOPS = (
-    ((0, 5), (0, 11)),
-    ((0, 1), (0, 15), (5, 1), (5, 15), (-5, 1), (-5, 15), (-5, 3)),
-    ((-1, 1), (4, 1), (-6, 1), (1, 15), (-4, 15), (6, 15)),
+    ((0, 3), (0, 13), (0, 6), (0, 10)),
+    ((0, 1), (0, 15), (3, 1), (-3, 15), (3, 15), (-3, 1), (6, 1), (-6, 15), (6, 15), (-6, 1), (-6, 2)),
 )
-GROUPS = ((0,), (5, -5), (1, -1, 4, -4, 6, -6, 8), (2, -2, 3, -3, 7, -7))
-Y_FIRST = (6, -6, 8, 7, -7, 3)
+GROUPS = ((0,), (3, -3, 6, -6), (1, -1, 2, -2, 4), (-4, 5, -5, 7, -7, 8))
+ORDER = (8, 7, 9, 6, 10, 5, 11, 4, 12, 3, 13, 2, 14, 1, 15, 0)
+
+
+def group_at(far, by):
+    landed_far = (far - by + 7) % Z - 7
+    return next(index for index, group in enumerate(GROUPS) if landed_far in group)
 
 
 def whole_wait(ref, sem):
@@ -38,11 +42,11 @@
     base_out, momentum_out, keys_out, weight_out, gain_out,
     codes, scales, base, momentum, inputs, cotangent, new_base, new_momentum, keys, grad_weight,
     decoded, twin_part, pairs, pieces, averages, rows, weight, gains, halves, both, inverse,
-    normed, twin_normed, totals, landed, terms, key_total, key_twin,
+    inverse_row, normed, twin_normed, totals, landed, terms, key_total, key_twin, key_part,
     local_sem, out_sem, twin_send, twin_recv, piece_send, piece_recv,
     average_send, average_recv, average_twin_send, average_twin_recv,
-    half_send, half_recv, up_send, up_recv, gain_send, gain_recv, gain_z_send, gain_z_recv,
-    normed_send, normed_recv, key_send, key_recv, sum_send, sum_recv, wz_send, wz_recv,
+    half_send, half_recv, up_send, up_recv, row_send, row_recv, gain_z_send, gain_z_recv,
+    normed_send, normed_recv, key_send, key_recv, part_send, part_recv, sum_send, sum_recv, wz_send, wz_recv,
     first_send, first_recv, second_send, second_recv, third_recv,
 ):
     rep = lax.axis_index("rep")
@@ -66,8 +70,8 @@
         return ((chip + step) % 8) * 2 + core, shard
 
     ring = (along_z(1), along_z(15))
-    right, left, across = (at(x_to=(x + by) % 4) for by in (1, 3, 2))
-    north, south, over = (at(y_to=(y + by) % 4) for by in (1, 3, 2))
+    across = at(x_to=(x + 2) % 4)
+    north, south = (at(y_to=(y + by) % 4) for by in (1, 3))
     twin = at(core_to=1 - core)
     partner = at(x_to=x_hi * 2 + 1 - x_lo)
 
@@ -84,7 +88,7 @@
         return carry
 
     lax.fori_loop(1, 8, greet, 0)
-    near = [twin, right, left] + [along_z(by) for by in (1, 15, 5, 11, 3, 13)]
+    near = [twin, partner] + [along_z(by) for by in (1, 15, 2, 14, 3, 13, 6, 10)]
     for device in near:
         pl.semaphore_signal(barrier, inc=1, device_id=device, device_id_type=MESH)
 
@@ -132,12 +136,13 @@
         whole_wait(cols, local_sem.at[index])
         square = lax.fori_loop(index * 4, index * 4 + 4, squares, square)
     inv = lax.rsqrt(jnp.sum(square, axis=1, keepdims=True) * (1.0 / D) + 1e-05)
-    inverse[...] = jnp.broadcast_to(inv, (TOK, 128))
+    inverse[pl.ds(0, TOK)] = jnp.broadcast_to(inv, (TOK, 128))
+    inverse_row[0] = jnp.transpose(inverse[pl.ds(0, TOK)])[:8]
     whole_wait(cotangent, local_sem.at[4])
     for sub in range(SUBS):
         both[sub, 0] = (cotangent[:, sub * PART:(sub + 1) * PART].astype(F32) * inv).astype(BF16)
     own_gain = gain[...].astype(F32)
-    gains[pl.ds(z * 2 + x_lo, 1)] = own_gain.reshape(1, 1, OWN)
+    gains[pl.ds(z, 1)] = own_gain.reshape(1, 1, OWN)
 
     pl.semaphore_wait(barrier, 7 + len(near))
 
@@ -150,7 +155,7 @@
         send(both.at[sub, 0], both.at[sub, 1], up_send, up_recv.at[sub], partner)
 
     send(decoded.at[pl.ds((1 - core) * 8, 8)], twin_part, twin_send, twin_recv, twin)
-    send(gains.at[z * 2 + x_lo], gains.at[z * 2 + x_lo], gain_send, gain_recv, partner)
+    send(inverse_row.at[0], inverse_row.at[1], row_send, row_recv, partner)
     send_up(0)
     send_half(8)
     for sub in (2, 1, 3):
@@ -168,9 +173,16 @@
 
     lax.fori_loop(1, 8, send_piece, 0)
 
+    here = set()
+
+    def need_half(far):
+        if far not in here:
+            whole_wait(halves.at[far], half_recv.at[far])
+            here.add(far)
+
     def features(far):
         target = (z + far) % Z
-        whole_wait(halves.at[target], half_recv.at[far])
+        need_half(far)
         start = pl.multiple_of((x_lo * Z + target) * OWN, OWN)
         return jnp.concatenate([inputs[:, pl.ds(start, OWN)], halves[target]], axis=0)
 
@@ -202,15 +214,16 @@
     send_half(6)
     send_half(10)
 
+    def send_gains(level):
+        for far, by in HOPS[level]:
+            block = gains.at[(z + far + Z) % Z]
+            send(block, block, gain_z_send, gain_z_recv.at[level], along_z(by))
+
     def gain_event(level):
-        if level == 0:
-            whole_wait(gains.at[0], gain_recv)
-        else:
-            whole_wait(gains.at[pl.ds(0, 2 * len(GROUPS[level]))], gain_z_recv.at[level - 1])
-        if level < 3:
-            for far, by in HOPS[level]:
-                block = gains.at[pl.ds(((z + far + Z) % Z) * 2, 2)]
-                send(block, block, gain_z_send, gain_z_recv.at[level], along_z(by))
+        if level > 0:
+            whole_wait(gains.at[pl.ds(0, len(HOPS[level - 1]))], gain_z_recv.at[level - 1])
+        if level < 2:
+            send_gains(level)
 
     gain_event(0)
     term(7, 0)
@@ -219,8 +232,6 @@
         sum_unit(2, 1 - sub // 2, sub, fresh=True)
     send_half(5)
     send_half(11)
-    for sub in (0, 2, 1, 3):
-        sum_unit(2, sub // 2, sub)
 
     mine = pl.ds(pl.multiple_of(own * 64, 64), 64)
 
@@ -240,7 +251,7 @@
         moved = momentum_decay * momentum[mine, :] + average
         rows[...] = (base[mine, :] - outer_rate * (average + momentum_decay * moved)) * D ** (-0.5)
         for col in range(4):
-            weight[z, y, x, :, col * 128:(col + 1) * 128] = rows[pl.ds(col, 16, stride=4), :].astype(BF16)
+            weight[z, y, x_hi, :, col * 128:(col + 1) * 128] = rows[pl.ds(col, 16, stride=4), :].astype(BF16)
         send_z(0)
         send_first(0)
 
@@ -273,113 +284,100 @@
 
     def send_z(level):
         for far, by in HOPS[level]:
-            block = weight.at[slice_at(far), y, x]
-            send(block, block, wz_send, wz_recv.at[level], along_z(by))
-
-    def z_event(level):
-        whole_wait(weight.at[pl.ds(0, len(GROUPS[level + 1])), 0, 0], wz_recv.at[level])
-        if level < 2:
-            send_z(level + 1)
-        send_first(level + 1)
+            block = weight.at[slice_at(far), y, x_hi]
+            send(block, block, wz_send, wz_recv.at[group_at(far, by)], along_z(by))
+
+    def z_event(group):
+        whole_wait(weight.at[pl.ds(0, len(GROUPS[group])), 0, 0], wz_recv.at[group])
+        if group == 1:
+            send_z(1)
+        send_first(group)
 
     def send_first(group):
         for far in GROUPS[group]:
-            block = weight.at[slice_at(far), y, x]
-            for device in (north, south, over) if far in Y_FIRST else (right, left, across):
-                send(block, block, first_send, first_recv.at[group], device)
+            block = weight.at[slice_at(far), y, x_hi]
+            send(block, block, first_send, first_recv.at[group], across)
 
     def send_second(group):
-        whole_wait(weight.at[pl.ds(0, len(GROUPS[group])), 0, pl.ds(0, 3)], first_recv.at[group])
+        whole_wait(weight.at[pl.ds(0, len(GROUPS[group])), 0, 0], first_recv.at[group])
         for far in GROUPS[group]:
-            held = weight.at[slice_at(far)]
-            if far in Y_FIRST:
-                block, devices = held.at[:, x], (right, left)
-            else:
-                block, devices = held.at[y], (north, south)
-            for device in devices:
+            block = weight.at[slice_at(far), y]
+            for device in (north, south):
                 send(block, block, second_send, second_recv.at[group], device)
 
     def send_third(group):
         whole_wait(weight.at[pl.ds(0, len(GROUPS[group])), pl.ds(0, 2)], second_recv.at[group])
-        turns = [0, 0]
-        for far in GROUPS[group]:
-            held = weight.at[slice_at(far)]
-            kind = int(far in Y_FIRST)
-            way = turns[kind] % 2
-            turns[kind] += 1
-            if kind:
-                block, device = held.at[:, (x + 3 - 2 * way) % 4], (right, left)[way]
-            else:
-                block, device = held.at[(y + 3 - 2 * way) % 4], (north, south)[way]
-            send(block, block, second_send, third_recv.at[group], device)
+        for turn, far in enumerate(GROUPS[group]):
+            way = turn % 2
+            block = weight.at[slice_at(far), (y + 3 - 2 * way) % 4]
+            send(block, block, second_send, third_recv.at[group], (north, south)[way])
 
     def normalize(part):
-        def one(block, carry):
-            start = pl.multiple_of(block * OWN, OWN)
-            scale = jnp.concatenate([inverse[...]] * 2, axis=1)
-            feature = (block % Z) * 2 + block // Z
-            value = (inputs[:, pl.ds(start, OWN)].astype(F32) * scale * gains[feature]).astype(BF16)
-            normed[0, block] = value[:, :128]
-            normed[1, block] = value[:, 128:]
-            return carry
-
-        lax.fori_loop(part * 8, part * 8 + 8, one, 0)
-        blocks = pl.ds(part * 8, 8)
-        send(normed.at[1 - core, blocks], twin_normed.at[blocks], normed_send, normed_recv, twin)
-
-    def project(group, first=0, last=None):
-        if group == 0:
+        if part == 0:
+            whole_wait(inverse_row.at[1], row_recv)
+            inverse[pl.ds(TOK, TOK)] = jnp.transpose(jnp.broadcast_to(inverse_row[1, 0:1], (128, TOK)))
+        scale = jnp.concatenate([inverse[...]] * 2, axis=1)
+        for place in range(part * 4, part * 4 + 4):
+            value = (features(ORDER[place]).astype(F32) * scale * gains[slice_at(ORDER[place])]).astype(BF16)
+            normed[0, place] = value[:, :128]
+            normed[1, place] = value[:, 128:]
+        places = pl.ds(part * 4, 4)
+        send(normed.at[1 - core, places], twin_normed.at[places], normed_send, normed_recv, twin)
+
+    def project(half):
+        if half == 0:
             whole_wait(twin_normed, normed_recv)
-        if first == 0:
-            whole_wait(weight.at[pl.ds(0, len(GROUPS[group])), 0], third_recv.at[group])
-        total = key_total[...]
-        for far in GROUPS[group][first:last]:
-            at_z = slice_at(far)
-            cols = jnp.concatenate([
-                jnp.concatenate([held[lo * Z + at_z] for lo in range(2)], axis=1)
-                for held in (normed.at[core], twin_normed)
-            ], axis=0)
-            parts = [
-                weight[at_z, member // 2, (member % 2) * 2 + lo] for lo in range(2) for member in range(8)
-            ]
-            total = total + jnp.dot(cols, jnp.concatenate(parts, axis=0), preferred_element_type=F32)
-        key_total[...] = total
+            for group in range(len(GROUPS)):
+                whole_wait(weight.at[pl.ds(0, len(GROUPS[group])), 0], third_recv.at[group])
+        places = range(half * 8, half * 8 + 8)
+        cols = jnp.concatenate([
+            jnp.concatenate([normed[core, place] for place in places], axis=1),
+            jnp.concatenate([twin_normed[place] for place in places], axis=1),
+        ], axis=0)
+        held = jnp.concatenate([weight[slice_at(ORDER[place])].reshape(128, KV) for place in places], axis=0)
+        value = jnp.dot(cols, held, preferred_element_type=F32)
+        key_total[...] = value if half == 0 else key_total[...] + value
 
     def send_keys():
-        send(key_total.at[pl.ds(TOK, TOK)], key_twin, key_send, key_recv, twin)
-
-    key_total[...] = jnp.zeros_like(key_total)
+        send(key_total.at[pl.ds(2 * TOK, 2 * TOK)], key_twin, key_send, key_recv, twin)
+
+    def swap_keys():
+        whole_wait(key_twin, key_recv)
+        key_part[0] = (key_total[pl.ds(TOK, TOK)] + key_twin[pl.ds(TOK, TOK)]).astype(BF16)
+        send(key_part.at[0], key_part.at[1], part_send, part_recv, partner)
+
+    for sub in (0, 2):
+        sum_unit(2, sub // 2, sub)
+    start_weight()
+    for sub in (1, 3):
+        sum_unit(2, sub // 2, sub)
     plan = {
-        (2, 3): ((start_weight,), (gain_event, 1)),
-        (3, 1): ((z_event, 0), (gain_event, 2)),
-        (3, 2): ((send_second, 0), (send_averages,)),
-        (4, 0): ((z_event, 1), (send_second, 1)),
-        (4, 1): ((send_third, 0), (gain_event, 3)),
-        (4, 2): ((normalize, 0),),
-        (4, 3): ((z_event, 2), (send_third, 1)),
-        (5, 0): ((send_second, 2),),
-        (5, 1): ((normalize, 1), (swap_averages,)),
-        (5, 2): ((normalize, 2),),
+        (2, 3): ((gain_event, 1),),
+        (3, 1): ((send_averages,),),
+        (3, 2): ((z_event, 1),),
+        (3, 3): ((send_second, 0), (gain_event, 2)),
+        (4, 1): ((send_third, 0),),
+        (4, 2): ((send_second, 1),),
+        (4, 3): ((z_event, 2),),
+        (5, 0): ((z_event, 3),),
+        (5, 1): ((normalize, 0), (swap_averages,)),
+        (5, 2): ((send_second, 2), (send_third, 1)),
         (5, 3): ((send_second, 3),),
-        (6, 0): ((normalize, 3),),
+        (6, 0): ((normalize, 1),),
         (6, 1): ((outer_step,),),
-        (6, 2): ((send_third, 2),),
-        (6, 3): ((project, 0),),
-        (7, 0): ((project, 1),),
-        (7, 1): ((send_third, 3),),
-        (7, 2): ((project, 2, 0, 4),),
-        (7, 3): ((project, 2, 4),),
-        (8, 1): ((project, 3, 0, 3),),
-        (8, 2): ((project, 3, 3), (send_keys,)),
+        (6, 2): ((send_third, 2), (normalize, 2)),
+        (6, 3): ((send_third, 3),),
+        (7, 0): ((normalize, 3),),
+        (7, 3): ((project, 0),),
+        (8, 0): ((project, 1), (send_keys,)),
+        (8, 3): ((swap_keys,),),
     }
     for step in range(2, STEPS + 1):
         if step > 2:
             term(9 - step, 0)
             term(Z - (9 - step), 1)
-            if step < 8:
-                send_half(7 - step)
-                if step < 7:
-                    send_half(9 + step)
+            for far in ORDER[3 * step - 2:3 * step + 1]:
+                send_half(far)
         for sub in range(SUBS):
             if step > 2:
                 sum_unit(step, 0, (sub + SUBS // 2) % SUBS)
@@ -390,10 +388,10 @@
     term(0, 0)
     gain_col = jnp.transpose(jnp.broadcast_to(own_gain, (128, OWN)))
     dots = jnp.zeros((OWN, 128), F32)
-    whole_wait(key_twin, key_recv)
-    keys[...] = (key_total[:TOK] + key_twin[...]).astype(BF16)
+    whole_wait(key_part.at[1], part_recv)
+    keys[...] = (key_total[:TOK] + key_twin[:TOK] + key_part[1].astype(F32)).astype(BF16)
     pltpu.make_async_copy(keys, keys_out, out_sem.at[2]).start()
-    for sub in range(SUBS):
+    for sub in (0, 2, 1, 3):
         cols = slice(sub * PART, (sub + 1) * PART)
         value = terms[0, :, cols]
         for way in range(2):
@@ -402,7 +400,7 @@
         grad_weight[:, cols] = value * gain_col
         row = (new_base[pl.ds(sub, OWN, stride=4), :] * D ** (-0.5)).astype(BF16).astype(F32)
         dots = dots + row * value
-    pltpu.make_async_copy(grad_weight, weight_out, out_sem.at[3]).start()
+        pltpu.make_async_copy(grad_weight.at[:, cols], weight_out.at[:, cols], out_sem.at[3 + sub]).start()
     gain_out[...] = jnp.sum(jnp.transpose(dots), axis=0, keepdims=True)
 
     whole_wait(twin_part, twin_send)
@@ -411,29 +409,37 @@
     whole_wait(averages.at[pl.ds(0, 8)], average_twin_send)
     whole_wait(halves, half_send)
     whole_wait(both.at[:, 1], up_send)
-    whole_wait(gains.at[0], gain_send)
-    whole_wait(gains.at[pl.ds(0, 30)], gain_z_send)
+    whole_wait(inverse_row.at[1], row_send)
+    whole_wait(gains.at[pl.ds(0, 15)], gain_z_send)
     whole_wait(twin_normed, normed_send)
     whole_wait(key_twin, key_send)
+    whole_wait(key_part.at[1], part_send)
     for way in range(2):
         whole_wait(totals.at[way, 0, pl.ds(0, SUBS // 2)], sum_send.at[way, 0])
         whole_wait(totals.at[way, pl.ds(1, STEPS - 1)], sum_send.at[way, 1])
     whole_wait(weight.at[pl.ds(0, 15), 0, 0], wz_send)
-    whole_wait(weight.at[pl.ds(0, 3)], first_send)
+    whole_wait(weight.at[pl.ds(0, 2)], first_send)
     whole_wait(weight.at[pl.ds(0, 12)], second_send)
     for index, (src, dst) in enumerate((
-        (new_base, base_out), (new_momentum, momentum_out), (keys, keys_out), (grad_weight, weight_out),
+        (new_base, base_out), (new_momentum, momentum_out), (keys, keys_out),
     )):
         pltpu.make_async_copy(src, dst, out_sem.at[index]).wait()
+    for sub in range(SUBS):
+        cols = slice(sub * PART, (sub + 1) * PART)
+        pltpu.make_async_copy(grad_weight.at[:, cols], weight_out.at[:, cols], out_sem.at[3 + sub]).wait()
 
 
 def finish(*refs):
-    count = len(refs) // 2
-    sem = refs[-1]
-    for index in range(count):
-        pltpu.make_async_copy(refs[index], refs[count + index], sem.at[index]).start()
-    for index in range(count):
-        pltpu.make_async_copy(refs[index], refs[count + index], sem.at[index]).wait()
+    sources, results, held, sem = refs[:5], refs[5:10], refs[10:15], refs[15]
+    inward = [pltpu.make_async_copy(sources[index], held[index], sem.at[0, index]) for index in range(5)]
+    outward = [pltpu.make_async_copy(held[index], results[index], sem.at[1, index]) for index in range(5)]
+    for copy in inward:
+        copy.start()
+    for index in range(5):
+        inward[index].wait()
+        outward[index].start()
+    for copy in outward:
+        copy.wait()
 
 
 def shards(codes, scales, base, momentum, inputs, gain, cotangent):
@@ -469,22 +475,24 @@
             pltpu.VMEM((7, 64, 128), BF16),
             pltpu.VMEM((16, 64, 128), BF16),
             pltpu.VMEM((64, 128), F32),
-            pltpu.VMEM((Z, 4, 4, 16, KV), BF16),
-            pltpu.VMEM((2 * Z, 1, OWN), F32),
+            pltpu.VMEM((Z, 4, 2, 16, KV), BF16),
+            pltpu.VMEM((Z, 1, OWN), F32),
             pltpu.VMEM((Z, TOK, OWN), BF16),
             pltpu.VMEM((SUBS, 2, TOK, PART), BF16),
-            pltpu.VMEM((TOK, 128), F32),
-            pltpu.VMEM((2, 2 * Z, TOK, 128), BF16),
-            pltpu.VMEM((2 * Z, TOK, 128), BF16),
+            pltpu.VMEM((2 * TOK, 128), F32),
+            pltpu.VMEM((2, 8, TOK), F32),
+            pltpu.VMEM((2, Z, 2 * TOK, 128), BF16),
+            pltpu.VMEM((Z, 2 * TOK, 128), BF16),
             pltpu.VMEM((2, STEPS, SUBS, OWN, PART), BF16),
             pltpu.VMEM((2, STEPS, SUBS, OWN, PART), BF16),
             pltpu.VMEM((2, OWN, KV), F32),
+            pltpu.VMEM((4 * TOK, KV), F32),
             pltpu.VMEM((2 * TOK, KV), F32),
-            pltpu.VMEM((TOK, KV), F32),
-            dma((9,)), dma((4,)), dma, dma, dma, dma,
+            pltpu.VMEM((2, TOK, KV), BF16),
+            dma((9,)), dma((3 + SUBS,)), dma, dma, dma, dma,
             dma, dma, dma, dma,
-            dma, dma((Z,)), dma, dma((SUBS,)), dma, dma, dma, dma((3,)),
-            dma, dma, dma, dma, dma((2, 2)), dma((2, STEPS, SUBS)), dma, dma((3,)),
+            dma, dma((Z,)), dma, dma((SUBS,)), dma, dma, dma, dma((2,)),
+            dma, dma, dma, dma, dma, dma, dma((2, 2)), dma((2, STEPS, SUBS)), dma, dma((4,)),
             dma, dma((4,)), dma, dma((4,)), dma((4,)),
         ],
         compiler_params=pltpu.CompilerParams(
@@ -495,7 +503,9 @@
         inputs[0], gain, cotangent[0],
     )
     out = pl.pallas_call(
-        finish, out_shape=results, in_specs=[vmem] * 5, out_specs=[hbm] * 5, scratch_shapes=[dma((5,))],
+        finish, out_shape=results, in_specs=[hbm] * 5, out_specs=[hbm] * 5,
+        scratch_shapes=[pltpu.VMEM(result.shape, result.dtype) for result in results] + [dma((2, 5))],
+        compiler_params=pltpu.CompilerParams(vmem_limit_bytes=58 * 1024 * 1024),
     )(*out)
     new_base, new_momentum, keys, grad_weight, grad_gain = out
     return new_base.reshape(-1), new_momentum.reshape(-1), keys[None], grad_weight[None], grad_gain

time: 80.6 us -> 78.3 us (0.971)
  the two profiles are of different devices: /device:TPU:4 before, /device:TPU:1 now
where the time goes in v3:
time: 78.3 us; the launch traced here: 78.1 us
  Pallas kernels  77.5 us (99%)
    pallas_call x1, Pallas kernels, shards(): pl.pallas_call(kernel, out_shape=results, in_specs=[hbm] * 5 + [vmem, hbm...  75.2 us
    pallas_call x1, Pallas kernels, shards(): pl.pallas_call(finish, out_shape=results, in_specs=[hbm] * 5, out_specs=[...  2.31 us

profile of v3, /device:TPU:1, one launch (start us, length us, event | category | flops | bytes accessed | tf_op | source)
XLA Modules:
  0.0 78.1 jit_solution(3359841804220917087)
XLA Ops:
  0.6 75.2 %shard_map.110 = (f32[1024,128]{1,0:T(8,128)}, f32[1024,128]{1,0:T(8,128)}, bf16[128,512]{1,0:T(8,128)(2,1)}, f32[256,512]{1,0:T(8,128)}, f32[1,256]{1,0:T(1,128)}) custom-call(s32[1024,128]{1,0:T(8,128)} %bitcast.11, f32[16,128]{1,0:T(8,128)} %bitcast.15, f32[1024,128]{1,0:T(8,128)} %bitcast.12, f32[1024,128]{1,0:T(8,128)} %bitcast.13, ...), custom_call_target="tpu_custom_call" | custom-call | tf_op jit(solution)/shard_map/pallas_call | solution.py:456
  75.8 2.3 %shard_map.111 = (f32[1024,128]{1,0:T(8,128)}, f32[1024,128]{1,0:T(8,128)}, bf16[128,512]{1,0:T(8,128)(2,1)}, f32[256,512]{1,0:T(8,128)}, f32[1,256]{1,0:T(1,128)}) custom-call(f32[1024,128]{1,0:T(8,128)} %get-tuple-element.15.refs_0_, f32[1024,128]{1,0:T(8,128)} %get-tuple-element.16.refs_1_, bf16[128,512]{1,0:T(8,128)(2,1)} %get-tuple-element.17.refs_2_, ...), custom_call_target="tpu_custom_call" | custom-call | tf_op jit(solution)/shard_map/pallas_call | solution.py:505

commit v4 on v3

--- a/solution.py
+++ b/solution.py
@@ -353,8 +353,8 @@
         sum_unit(2, sub // 2, sub)
     plan = {
         (2, 3): ((gain_event, 1),),
-        (3, 1): ((send_averages,),),
-        (3, 2): ((z_event, 1),),
+        (3, 1): ((z_event, 1),),
+        (3, 2): ((send_averages,),),
         (3, 3): ((send_second, 0), (gain_event, 2)),
         (4, 1): ((send_third, 0),),
         (4, 2): ((send_second, 1),),

time: 78.3 us -> 79 us (level)
  no operation moved by 1% of the time
where the time goes in v4:
time: 79 us; the launch traced here: 78.9 us
  Pallas kernels  78.2 us (99%)
    pallas_call x1, Pallas kernels, shards(): pl.pallas_call(kernel, out_shape=results, in_specs=[hbm] * 5 + [vmem, hbm...  75.9 us
    pallas_call x1, Pallas kernels, shards(): pl.pallas_call(finish, out_shape=results, in_specs=[hbm] * 5, out_specs=[...  2.31 us

profile of v4, /device:TPU:1, one launch (start us, length us, event | category | flops | bytes accessed | tf_op | source)
XLA Modules:
  0.0 78.9 jit_solution(8128699728009321544)
XLA Ops:
  0.6 75.9 %shard_map.110 = (f32[1024,128]{1,0:T(8,128)}, f32[1024,128]{1,0:T(8,128)}, bf16[128,512]{1,0:T(8,128)(2,1)}, f32[256,512]{1,0:T(8,128)}, f32[1,256]{1,0:T(1,128)}) custom-call(s32[1024,128]{1,0:T(8,128)} %bitcast.11, f32[16,128]{1,0:T(8,128)} %bitcast.15, f32[1024,128]{1,0:T(8,128)} %bitcast.12, f32[1024,128]{1,0:T(8,128)} %bitcast.13, ...), custom_call_target="tpu_custom_call" | custom-call | tf_op jit(solution)/shard_map/pallas_call | solution.py:456
  76.6 2.3 %shard_map.111 = (f32[1024,128]{1,0:T(8,128)}, f32[1024,128]{1,0:T(8,128)}, bf16[128,512]{1,0:T(8,128)(2,1)}, f32[256,512]{1,0:T(8,128)}, f32[1,256]{1,0:T(1,128)}) custom-call(f32[1024,128]{1,0:T(8,128)} %get-tuple-element.15.refs_0_, f32[1024,128]{1,0:T(8,128)} %get-tuple-element.16.refs_1_, bf16[128,512]{1,0:T(8,128)(2,1)} %get-tuple-element.17.refs_2_, ...), custom_call_target="tpu_custom_call" | custom-call | tf_op jit(solution)/shard_map/pallas_call | solution.py:505
